TPU v7x, 512 devices: a whole 4x8x8 slice. The times are simulated.
512 devices in a mesh: mem: 16 (over z, y_lo), lon: 32 (over y_hi, x, core).
Axes of the slice: x: 4, y: 8 (y_hi: 4, y_lo: 2; y = y_hi * 2 + y_lo), z: 8, core: 2. Of those that a mesh axis runs over, the one named last changes fastest.
Arguments:
- fields: bfloat16 [80, 64, 256, 128], P('mem', None, 'lon'), may hold values from -8 to 8
- w_query: bfloat16 [24, 576], replicated, may hold values from -1 to 1
- w_key: bfloat16 [24, 576], replicated, may hold values from -1 to 1
- w_value: bfloat16 [24, 576], replicated, may hold values from -0.25 to 0.25
- w_out: bfloat16 [64, 216], replicated, may hold values from -1.25 to 1.25
Outputs:
- updated: bfloat16 [80, 64, 256, 128], P('mem', None, 'lon')
All inputs are finite; a program needn't handle non-finite values.
Results may differ from a plain program's by a relative error of at most 0.008.
Values may be sent and summed in bfloat16 or wider, within the bound.
No kernel may reach another device: no remote copies, remote signals or barrier semaphores. Data moves between devices by JAX's collectives and lax.ppermute only.
A program may use at most 64 MiB of HBM per device.

v0:
```python
import math
import jax
import jax.numpy as jnp
from jax import lax
from jax.sharding import PartitionSpec as P


def with_halo(block, sides, width):
    for axis, dim in sides:
        count = lax.axis_size(axis)
        forward = [(i, i + 1) for i in range(count - 1)]
        forward.append((count - 1, 0))
        backward = [(target, source) for source, target in forward]
        low = lax.ppermute(
            lax.slice_in_dim(block, block.shape[dim] - width, None, axis=dim), axis, forward
        )
        high = lax.ppermute(lax.slice_in_dim(block, 0, width, axis=dim), axis, backward)
        block = jnp.concatenate([low, block, high], axis=dim)
    return block


def tap_stack(extended):
    span_lon = extended.shape[2] - 2
    latitudes = extended.shape[3]
    padded = jnp.pad(extended, ((0, 0), (0, 0), (0, 0), (1, 1)))
    return jnp.concatenate(
        [
            padded[:, :, lon_step : lon_step + span_lon, lat_step : lat_step + latitudes]
            for lon_step in range(3)
            for lat_step in range(3)
        ],
        axis=1,
    )


def shards(fields, w_query, w_key, w_value, w_out):
    members = fields.shape[0]
    longitudes = fields.shape[2]
    latitudes = fields.shape[3]
    inner_width = w_query.shape[0]
    extended = with_halo(fields, (("lon", 2),), 1)
    w_inner = jnp.concatenate([w_query, w_key, w_value], axis=0)
    projected = jnp.einsum(
        "oc,mcwh->mowh", w_inner, tap_stack(extended), preferred_element_type=jnp.float32
    ).astype(jnp.bfloat16)
    queries = projected[:, :inner_width]
    keys_local = projected[:, inner_width : 2 * inner_width]
    values = projected[:, 2 * inner_width :]
    query_blocks, key_blocks = (
        lax.all_to_all(queries, "mem", split_axis=3, concat_axis=0, tiled=True),
        lax.all_to_all(keys_local, "mem", split_axis=3, concat_axis=0, tiled=True),
    )
    total_members = query_blocks.shape[0]
    partial_value = jnp.dot(
        query_blocks.reshape(total_members, -1),
        key_blocks.reshape(total_members, -1).T,
        preferred_element_type=jnp.float32,
    )
    score_scale = 1.0 / math.sqrt(inner_width * latitudes * longitudes * lax.axis_size("lon"))
    first_row = lax.axis_index("mem") * members
    gram_sums = lax.psum(partial_value, ("mem", "lon"))
    weights_all = jax.nn.softmax(gram_sums * score_scale, axis=1).astype(jnp.bfloat16)
    weights_own = lax.dynamic_slice_in_dim(weights_all, first_row, members, 0)
    mixed_values = jnp.einsum(
        "mn,ncwh->mcwh",
        weights_own,
        lax.all_gather(values, "mem", axis=0, tiled=True),
        preferred_element_type=jnp.float32,
    ).astype(jnp.bfloat16)
    mixed_ext = with_halo(mixed_values, (("lon", 2),), 1)
    branch = jnp.einsum(
        "oc,mcwh->mowh", w_out, tap_stack(mixed_ext), preferred_element_type=jnp.float32
    )
    return (fields.astype(jnp.float32) + branch).astype(jnp.bfloat16)


def solution(mesh):
    return jax.shard_map(
        shards,
        mesh=mesh,
        in_specs=(P("mem", None, "lon", None), P(), P(), P(), P()),
        out_specs=P("mem", None, "lon", None),
        check_vma=False,
    )
```

profile of v0, /device:TPU:23, one launch (start us, length us, event | category | flops | bytes accessed | tf_op | source)
XLA Modules:
  0.0 210.7 jit_solution(2268765919190541490)
XLA Ops:
  6.5 1.2 copy.30
  7.8 5.9 %collective-permute-start = (bf16[5,64,1,128]{3,1,2,0:T(8,128)(2,1)S(1)}, bf16[5,64,1,128]{3,1,2,0:T(8,128)(2,1)S(1)}, u32[]{:S(2)}, u32[]{:S(2)}) collective-permute-start(bf16[5,64,1,128]{3,1,2,0:T(8,128)(2,1)S(1)} %get-tuple-element.10), channel_id=1, source_target_pairs={{0,1},{1,2},{2,3},{3,4},{4,5},{5,6},{6,7},{7,8},{8,9},{9,10},{10,1... | collective-permute-start | bytes 245768 | tf_op jit(solution)/shard_map/ppermute | solution.py:14
  13.7 2.1 collective-permute-start.1
  15.8 8.9 %collective-permute-done.1 = bf16[5,64,1,128]{3,1,2,0:T(8,128)(2,1)S(1)} collective-permute-done((bf16[5,64,1,128]{3,1,2,0:T(8,128)(2,1)S(1)}, bf16[5,64,1,128]{3,1,2,0:T(8,128)(2,1)S(1)}, u32[]{:S(2)}, u32[]{:S(2)}) %collective-permute-start.1) | collective-permute-done | bytes 81952 | tf_op jit(solution)/shard_map/ppermute | solution.py:17
  24.7 0.9 fusion.10
  27.7 1.2 fusion.20
  30.4 2.4 %reshape.15 = bf16[16,2,3840]{2,1,0:T(2,128)(2,1)} reshape(bf16[128,5,8,24]{3,2,1,0:T(8,128)(2,1)S(1)} %bitcast.42) | data formatting | bytes 491520
  32.9 10.2 %all-to-all-start = ((bf16[16,2,3840]{2,1,0:T(2,128)(2,1)}), bf16[16,2,3840]{2,1,0:T(2,128)(2,1)S(1)}, u32[]{:S(2)}, u32[]{:S(2)}) async-start(bf16[16,2,3840]{2,1,0:T(2,128)(2,1)} %reshape.15), calls=%async_computation | async-start | bytes 491520 | tf_op jit(solution)/shard_map/all_to_all | solution.py:50
  43.7 2.5 %reshape.17 = bf16[16,2,3840]{2,1,0:T(2,128)(2,1)} reshape(bf16[128,5,8,24]{3,2,1,0:T(8,128)(2,1)S(1)} %bitcast.43) | data formatting | bytes 491520
  46.2 5.6 %all-to-all-done = bf16[16,2,3840]{2,1,0:T(2,128)(2,1)S(1)} async-done(((bf16[16,2,3840]{2,1,0:T(2,128)(2,1)}), bf16[16,2,3840]{2,1,0:T(2,128)(2,1)S(1)}, u32[]{:S(2)}, u32[]{:S(2)}) %all-to-all-start) | async-done | bytes 245792 | tf_op jit(solution)/shard_map/all_to_all | solution.py:50
  51.8 4.0 %all-to-all-start.1 = ((bf16[16,2,3840]{2,1,0:T(2,128)(2,1)}), bf16[16,2,3840]{2,1,0:T(2,128)(2,1)S(1)}, u32[]{:S(2)}, u32[]{:S(2)}) async-start(bf16[16,2,3840]{2,1,0:T(2,128)(2,1)} %reshape.17), calls=%async_computation.1 | async-start | bytes 491520 | tf_op jit(solution)/shard_map/all_to_all | solution.py:51
  55.8 1.8 reshape.16
  57.7 3.6 %copy.39 = bf16[16,5,24,8,8]{4,3,2,1,0:T(8,128)(2,1)} copy(bf16[16,5,24,8,8]{2,3,1,4,0:T(8,128)(2,1)S(1)} %bitcast.40) | data formatting | bytes 491520 | tf_op jit(solution)/shard_map/all_to_all | solution.py:50
  61.3 6.3 %reshape.10 = bf16[80,1536]{1,0:T(8,128)(2,1)S(1)} reshape(bf16[16,5,24,8,8]{4,3,2,1,0:T(8,128)(2,1)} %copy.39) | data formatting | bytes 491520 | tf_op jit(solution)/shard_map/reshape | solution.py:55
  67.6 1.8 reshape.18
  69.5 3.6 %copy.42 = bf16[16,5,24,8,8]{4,3,2,1,0:T(8,128)(2,1)} copy(bf16[16,5,24,8,8]{2,3,1,4,0:T(8,128)(2,1)S(1)} %bitcast.41) | data formatting | bytes 491520 | tf_op jit(solution)/shard_map/all_to_all | solution.py:51
  73.1 6.3 %reshape.11 = bf16[80,1536]{1,0:T(8,128)(2,1)S(1)} reshape(bf16[16,5,24,8,8]{4,3,2,1,0:T(8,128)(2,1)} %copy.42) | data formatting | bytes 491520 | tf_op jit(solution)/shard_map/reshape | solution.py:56
  79.6 96.1 %psum.7 = f32[80,80]{1,0:T(8,128)S(1)} all-reduce(f32[80,80]{1,0:T(8,128)S(1)} %fusion.47), channel_id=1, replica_groups=mesh['mem'=16,'lon'=32] {'mem','lon'}, use_global_device_ids=true, to_apply=%region_0.1 | all-reduce | flops 6400 | bytes 51200 | tf_op jit(solution)/shard_map/psum | solution.py:61
  176.1 4.3 %fusion.21 = bf16[5,24,8,128]{3,0,2,1:T(8,128)(2,1)S(1)} fusion(bf16[80,24,8,128]{3,2,1,0:T(8,128)(2,1)} %all-gather.2.cloned.1.call-done, f32[80,80]{1,0:T(8,128)S(1)} %get-tuple-element.6, s32[]{:T(128)S(6)} %select_n.3, f32[5]{0:T(128)S(1)} %dynamic-slice), kind=kOutput, calls=%fused_computation.20 | convolution fusion | flops 19784480 | bytes 4182532 | tf_op jit(solution)/shard_map/mn,ncwh->mcwh/dot_general | solution.py:64
  180.4 7.6 %collective-permute-start.2 = (bf16[5,24,1,128]{3,0,2,1:T(8,128)(2,1)S(1)}, bf16[5,24,1,128]{3,0,2,1:T(8,128)(2,1)S(1)}, u32[]{:S(2)}, u32[]{:S(2)}) collective-permute-start(bf16[5,24,1,128]{3,0,2,1:T(8,128)(2,1)S(1)} %get-tuple-element.12), channel_id=1, source_target_pairs={{0,1},{1,2},{2,3},{3,4},{4,5},{5,6},{6,7},{7,8},{8,9},{9,10},{10,1... | collective-permute-start | bytes 92168 | tf_op jit(solution)/shard_map/ppermute | solution.py:14
  188.0 2.1 %collective-permute-start.3 = (bf16[5,24,1,128]{3,0,2,1:T(8,128)(2,1)S(1)}, bf16[5,24,1,128]{3,0,2,1:T(8,128)(2,1)S(1)}, u32[]{:S(2)}, u32[]{:S(2)}) collective-permute-start(bf16[5,24,1,128]{3,0,2,1:T(8,128)(2,1)S(1)} %get-tuple-element.13), channel_id=1, source_target_pairs={{1,0},{2,1},{3,2},{4,3},{5,4},{6,5},{7,6},{8,7},{9,8},{10,9},{11,1... | collective-permute-start | bytes 92168 | tf_op jit(solution)/shard_map/ppermute | solution.py:17
  190.1 7.9 %collective-permute-done.3 = bf16[5,24,1,128]{3,0,2,1:T(8,128)(2,1)S(1)} collective-permute-done((bf16[5,24,1,128]{3,0,2,1:T(8,128)(2,1)S(1)}, bf16[5,24,1,128]{3,0,2,1:T(8,128)(2,1)S(1)}, u32[]{:S(2)}, u32[]{:S(2)}) %collective-permute-start.3) | collective-permute-done | bytes 30752 | tf_op jit(solution)/shard_map/ppermute | solution.py:17
  200.0 2.6 %fusion.17 = bf16[5,64,8,128]{3,1,2,0:T(8,128)(2,1)S(1)} fusion(bf16[5,216,8,128]{3,0,2,1:T(8,128)(2,1)S(1)} %slice_dynamic-update-slice_fusion.6, bf16[64,216]{1,0:T(8,128)(2,1)S(1)} %copy-done, bf16[5,64,8,128]{3,2,1,0:T(8,128)(2,1)S(1)} %copy-done.1), kind=kOutput, calls=%fused_computation.18 | convolution fusion | flops 142540800 | bytes 3550208 | tf_op jit(solution)/shard_map/oc,mcwh->mowh/dot_general | solution.py:71
  202.6 1.3 copy.46
  (45 shorter events, 6.6 us)
Async XLA Ops:
  6.5 193.4 %copy-start = (bf16[64,216]{1,0:T(8,128)(2,1)S(1)}, bf16[64,216]{1,0:T(8,128)(2,1)}, u32[]{:S(2)}) copy-start(bf16[64,216]{1,0:T(8,128)(2,1)} %param.9) | copy-start | bytes 82948
  6.5 169.5 %all-gather.2.cloned.1.call-start = ((), (), s32[]{:S(2)}) async-start(), calls=%async_computation.2 | async-start | bytes 4177920 | tf_op jit(solution)/shard_map/all_gather | solution.py:67
  7.8 8.0 %collective-permute-start = (bf16[5,64,1,128]{3,1,2,0:T(8,128)(2,1)S(1)}, bf16[5,64,1,128]{3,1,2,0:T(8,128)(2,1)S(1)}, u32[]{:S(2)}, u32[]{:S(2)}) collective-permute-start(bf16[5,64,1,128]{3,1,2,0:T(8,128)(2,1)S(1)} %get-tuple-element.10), channel_id=1, source_target_pairs={{0,1},{1,2},{2,3},{3,4},{4,5},{5,6},{6,7},{7,8},{8,9},{9,10},{10,1... | collective-permute-start | bytes 245768 | tf_op jit(solution)/shard_map/ppermute | solution.py:14
  13.7 12.7 %copy-start.1 = (bf16[5,64,8,128]{3,2,1,0:T(8,128)(2,1)S(1)}, bf16[5,64,8,128]{3,2,1,0:T(8,128)(2,1)}, u32[]{:S(2)}) copy-start(bf16[5,64,8,128]{3,2,1,0:T(8,128)(2,1)} %param.5) | copy-start | bytes 1966084
  13.7 11.0 %collective-permute-start.1 = (bf16[5,64,1,128]{3,1,2,0:T(8,128)(2,1)S(1)}, bf16[5,64,1,128]{3,1,2,0:T(8,128)(2,1)S(1)}, u32[]{:S(2)}, u32[]{:S(2)}) collective-permute-start(bf16[5,64,1,128]{3,1,2,0:T(8,128)(2,1)S(1)} %get-tuple-element.11), channel_id=1, source_target_pairs={{1,0},{2,1},{3,2},{4,3},{5,4},{6,5},{7,6},{8,7},{9,8},{10,9},{11,1... | collective-permute-start | bytes 245768 | tf_op jit(solution)/shard_map/ppermute | solution.py:17
  26.4 1.3 copy-start.2
  26.4 1.3 copy-start.3
  26.4 1.3 copy-start.4
  32.9 18.9 %all-to-all-start = ((bf16[16,2,3840]{2,1,0:T(2,128)(2,1)}), bf16[16,2,3840]{2,1,0:T(2,128)(2,1)S(1)}, u32[]{:S(2)}, u32[]{:S(2)}) async-start(bf16[16,2,3840]{2,1,0:T(2,128)(2,1)} %reshape.15), calls=%async_computation | async-start | bytes 491520 | tf_op jit(solution)/shard_map/all_to_all | solution.py:50
  51.8 15.8 %all-to-all-start.1 = ((bf16[16,2,3840]{2,1,0:T(2,128)(2,1)}), bf16[16,2,3840]{2,1,0:T(2,128)(2,1)S(1)}, u32[]{:S(2)}, u32[]{:S(2)}) async-start(bf16[16,2,3840]{2,1,0:T(2,128)(2,1)} %reshape.17), calls=%async_computation.1 | async-start | bytes 491520 | tf_op jit(solution)/shard_map/all_to_all | solution.py:51
  180.4 9.7 %collective-permute-start.2 = (bf16[5,24,1,128]{3,0,2,1:T(8,128)(2,1)S(1)}, bf16[5,24,1,128]{3,0,2,1:T(8,128)(2,1)S(1)}, u32[]{:S(2)}, u32[]{:S(2)}) collective-permute-start(bf16[5,24,1,128]{3,0,2,1:T(8,128)(2,1)S(1)} %get-tuple-element.12), channel_id=1, source_target_pairs={{0,1},{1,2},{2,3},{3,4},{4,5},{5,6},{6,7},{7,8},{8,9},{9,10},{10,1... | collective-permute-start | bytes 92168 | tf_op jit(solution)/shard_map/ppermute | solution.py:14
  188.0 10.1 %collective-permute-start.3 = (bf16[5,24,1,128]{3,0,2,1:T(8,128)(2,1)S(1)}, bf16[5,24,1,128]{3,0,2,1:T(8,128)(2,1)S(1)}, u32[]{:S(2)}, u32[]{:S(2)}) collective-permute-start(bf16[5,24,1,128]{3,0,2,1:T(8,128)(2,1)S(1)} %get-tuple-element.13), channel_id=1, source_target_pairs={{1,0},{2,1},{3,2},{4,3},{5,4},{6,5},{7,6},{8,7},{9,8},{10,9},{11,1... | collective-permute-start | bytes 92168 | tf_op jit(solution)/shard_map/ppermute | solution.py:17
Sparse Core Ops, SparseCore 0:
  29.9 102.4 all-gather.1
where the time goes:
time: 211 us
  blocking collectives  96.1 us (46%)
  local copies, waits for them, and re-layouts  36.1 us (17%)
  starting transfers between devices  31.8 us (15%)
  waiting for transfers between devices  22.5 us (11%)
  between operations  13.8 us (7%)
  matrix products  8.3 us (4%)
  other arithmetic  2.14 us (1%)
    psum x1, blocking collectives, shards(): gram_sums = lax.psum(partial_value, ('mem', 'lon'))  96.1 us
    ppermute x2, waiting for transfers between devices, with_halo(): lax.ppermute(lax.slice_in_dim(block, 0, width, axis=dim), axis, backward)  16.8 us
    ppermute x2, starting transfers between devices, with_halo(): lax.ppermute(lax.slice_in_dim(block, block.shape[dim] - width, None, axis...  13.5 us
    unnamed x27, local copies, waits for them, and re-layouts  12.1 us
    all_to_all x1, starting transfers between devices, shards(): lax.all_to_all(queries, 'mem', split_axis=3, concat_axis=0, tiled=True)  10.2 us
    reshape x1, local copies, waits for them, and re-layouts, shards(): query_blocks.reshape(total_members, -1)  6.3 us
    reshape x1, local copies, waits for them, and re-layouts, shards(): key_blocks.reshape(total_members, -1)  6.29 us
    all_to_all x1, waiting for transfers between devices, shards(): lax.all_to_all(queries, 'mem', split_axis=3, concat_axis=0, tiled=True)  5.63 us
  transfers between devices with their start and end apart: 7, of which 3 were waited for; matrix products, arithmetic and copies ran while one was open for 14% of the time, Pallas kernels for 0%

commit v1 on v0

--- a/solution.py
+++ b/solution.py
@@ -48,7 +48,12 @@
     values = projected[:, 2 * inner_width :]
     query_blocks, key_blocks = (
         lax.all_to_all(queries, "mem", split_axis=3, concat_axis=0, tiled=True),
-        lax.all_to_all(keys_local, "mem", split_axis=3, concat_axis=0, tiled=True),
+        jnp.concatenate(
+            lax.all_to_all(
+                jnp.stack(jnp.split(keys_local, lax.axis_size("mem"), axis=3)), "mem", 0, 0
+            ),
+            axis=0,
+        ),
     )
     total_members = query_blocks.shape[0]
     partial_value = jnp.dot(

time: 211 us -> 224 us (1.062)
  local copies, waits for them, and re-layouts: 36.1 us -> 48.3 us
    another operation x0 -> x19, local copies, waits for them, and re-layouts: none -> 17.9 us  [the longest x18 11.7 us: shards(): jnp.stack(jnp.split(keys_local, lax.axis_size('mem'), axis=3))]
    all_to_all x1, waiting for transfers between devices: 0.01 us -> 6.78 us  [shards(): lax.all_to_all(jnp.stack(jnp.split(keys_local, lax.axis_size('mem'), axis...]
    all_to_all x1, starting transfers between devices: 10.2 us -> 3.71 us  [shards(): lax.all_to_all(queries, 'mem', split_axis=3, concat_axis=0, tiled=True)]
    reshape x1 -> x0, local copies, waits for them, and re-layouts: 6.29 us -> none  [shards(): key_blocks.reshape(total_members, -1)]
    all_to_all x1, starting transfers between devices: 4.01 us -> 10.1 us  [shards(): lax.all_to_all(jnp.stack(jnp.split(keys_local, lax.axis_size('mem'), axis...]
    all_to_all x1, waiting for transfers between devices: 5.63 us -> 0.01 us  [shards(): lax.all_to_all(queries, 'mem', split_axis=3, concat_axis=0, tiled=True)]
    unnamed x27 -> x52, local copies, waits for them, and re-layouts: 12.1 us -> 12.9 us
  transfers between devices with their start and end apart: 7 -> 7, of which waited for: 3 -> 3; matrix products, arithmetic and copies ran while one was open for 14% -> 19% of each run, Pallas kernels for 0% -> 0%
where the time goes in v1:
time: 224 us
  blocking collectives  96.1 us (43%)
  local copies, waits for them, and re-layouts  48.3 us (22%)
  starting transfers between devices  31.4 us (14%)
  waiting for transfers between devices  23.3 us (10%)
  between operations  13.9 us (6%)
  matrix products  8.31 us (4%)
    psum x1, blocking collectives, shards(): gram_sums = lax.psum(partial_value, ('mem', 'lon'))  96.1 us
    ppermute x2, waiting for transfers between devices, with_halo(): lax.ppermute(lax.slice_in_dim(block, 0, width, axis=dim), axis, backward)  16.5 us
    ppermute x2, starting transfers between devices, with_halo(): lax.ppermute(lax.slice_in_dim(block, block.shape[dim] - width, None, axis...  13.5 us
    unnamed x52, local copies, waits for them, and re-layouts  12.9 us
    another operation x18, local copies, waits for them, and re-layouts, shards(): jnp.stack(jnp.split(keys_local, lax.axis_size('mem'), axis=3))  11.7 us
    all_to_all x1, starting transfers between devices, shards(): lax.all_to_all(jnp.stack(jnp.split(keys_local, lax.axis_size('mem'), axis...  10.1 us
    all_to_all x1, waiting for transfers between devices, shards(): lax.all_to_all(jnp.stack(jnp.split(keys_local, lax.axis_size('mem'), axis...  6.78 us
    another operation x1, local copies, waits for them, and re-layouts, shards(): key_blocks.reshape(total_members, -1)  6.28 us
  transfers between devices with their start and end apart: 7, of which 3 were waited for; matrix products, arithmetic and copies ran while one was open for 19% of the time, Pallas kernels for 0%

profile of v1, /device:TPU:23, one launch (start us, length us, event | category | flops | bytes accessed | tf_op | source)
XLA Modules:
  0.0 223.5 jit_solution(4656500957719286019)
XLA Ops:
  7.8 5.9 %collective-permute-start = (bf16[5,64,1,128]{3,1,2,0:T(8,128)(2,1)S(1)}, bf16[5,64,1,128]{3,1,2,0:T(8,128)(2,1)S(1)}, u32[]{:S(2)}, u32[]{:S(2)}) collective-permute-start(bf16[5,64,1,128]{3,1,2,0:T(8,128)(2,1)S(1)} %get-tuple-element.25), channel_id=1, source_target_pairs={{0,1},{1,2},{2,3},{3,4},{4,5},{5,6},{6,7},{7,8},{8,9},{9,10},{10,1... | collective-permute-start | bytes 245768 | tf_op jit(solution)/shard_map/ppermute | solution.py:14
  13.7 1.9 collective-permute-start.1
  15.7 8.9 %collective-permute-done.1 = bf16[5,64,1,128]{3,1,2,0:T(8,128)(2,1)S(1)} collective-permute-done((bf16[5,64,1,128]{3,1,2,0:T(8,128)(2,1)S(1)}, bf16[5,64,1,128]{3,1,2,0:T(8,128)(2,1)S(1)}, u32[]{:S(2)}, u32[]{:S(2)}) %collective-permute-start.1) | collective-permute-done | bytes 81952 | tf_op jit(solution)/shard_map/ppermute | solution.py:17
  30.8 2.3 %slice_bitcast_fusion = (bf16[1,5,24,8,8]{4,2,3,1,0:T(8,128)(2,1)S(1)}, bf16[1,5,24,8,8]{4,2,3,1,0:T(8,128)(2,1)S(1)}, bf16[1,5,24,8,8]{4,2,3,1,0:T(8,128)(2,1)S...) fusion(bf16[5,72,8,128]{3,1,2,0:T(8,128)(2,1)S(1)} %fusion.20), kind=kLoop, calls=%fused_computation.46 | loop fusion | bytes 491520 | tf_op jit(solution)/shard_map/stack | solution.py:53
  33.1 1.8 copy.39
  34.9 1.7 copy.40
  42.9 2.4 %reshape.12 = bf16[16,2,3840]{2,1,0:T(2,128)(2,1)} reshape(bf16[16,5,8,8,24]{4,3,2,1,0:T(8,128)(2,1)S(1)} %bitcast.72) | data formatting | bytes 491520
  45.4 10.1 %all-to-all-start.1 = ((bf16[16,2,3840]{2,1,0:T(2,128)(2,1)}), bf16[16,2,3840]{2,1,0:T(2,128)(2,1)S(1)}, u32[]{:S(2)}, u32[]{:S(2)}) async-start(bf16[16,2,3840]{2,1,0:T(2,128)(2,1)} %reshape.12), calls=%async_computation.1 | async-start | bytes 491520 | tf_op jit(solution)/shard_map/all_to_all | solution.py:52
  56.2 2.4 %reshape.10 = bf16[16,2,3840]{2,1,0:T(2,128)(2,1)} reshape(bf16[128,5,8,24]{3,2,1,0:T(8,128)(2,1)S(1)} %bitcast.71) | data formatting | bytes 491520
  58.6 6.8 %all-to-all-done.1 = bf16[16,2,3840]{2,1,0:T(2,128)(2,1)S(1)} async-done(((bf16[16,2,3840]{2,1,0:T(2,128)(2,1)}), bf16[16,2,3840]{2,1,0:T(2,128)(2,1)S(1)}, u32[]{:S(2)}, u32[]{:S(2)}) %all-to-all-start.1) | async-done | bytes 245792 | tf_op jit(solution)/shard_map/all_to_all | solution.py:52
  65.4 3.7 %all-to-all-start = ((bf16[16,2,3840]{2,1,0:T(2,128)(2,1)}), bf16[16,2,3840]{2,1,0:T(2,128)(2,1)S(1)}, u32[]{:S(2)}, u32[]{:S(2)}) async-start(bf16[16,2,3840]{2,1,0:T(2,128)(2,1)} %reshape.10), calls=%async_computation | async-start | bytes 491520 | tf_op jit(solution)/shard_map/all_to_all | solution.py:50
  69.1 1.8 reshape.13
  71.0 3.5 %copy.55 = bf16[16,5,24,8,8]{4,3,2,1,0:T(8,128)(2,1)} copy(bf16[16,5,24,8,8]{2,4,3,1,0:T(8,128)(2,1)S(1)} %bitcast.69) | data formatting | bytes 491520 | tf_op jit(solution)/shard_map/all_to_all | solution.py:52
  74.5 6.3 %reshape_reshape.3 = bf16[80,1536]{1,0:T(8,128)(2,1)S(1)} reshape(bf16[16,5,24,8,8]{4,3,2,1,0:T(8,128)(2,1)} %copy.55) | data formatting | bytes 491520 | tf_op jit(solution)/shard_map/reshape;reshape | solution.py:61
  80.8 1.8 reshape.11
  82.6 3.6 %copy.38 = bf16[16,5,24,8,8]{4,3,2,1,0:T(8,128)(2,1)} copy(bf16[16,5,24,8,8]{2,3,1,4,0:T(8,128)(2,1)S(1)} %bitcast.70) | data formatting | bytes 491520 | tf_op jit(solution)/shard_map/all_to_all | solution.py:50
  86.3 6.3 %reshape.6 = bf16[80,1536]{1,0:T(8,128)(2,1)S(1)} reshape(bf16[16,5,24,8,8]{4,3,2,1,0:T(8,128)(2,1)} %copy.38) | data formatting | bytes 491520 | tf_op jit(solution)/shard_map/reshape | solution.py:60
  92.8 96.1 %psum.7 = f32[80,80]{1,0:T(8,128)S(1)} all-reduce(f32[80,80]{1,0:T(8,128)S(1)} %fusion.47), channel_id=1, replica_groups=mesh['mem'=16,'lon'=32] {'mem','lon'}, use_global_device_ids=true, to_apply=%region_0.1 | all-reduce | flops 6400 | bytes 51200 | tf_op jit(solution)/shard_map/psum | solution.py:66
  189.2 4.3 %fusion.21 = bf16[5,24,8,128]{3,0,2,1:T(8,128)(2,1)S(1)} fusion(bf16[80,24,8,128]{3,2,1,0:T(8,128)(2,1)} %all-gather.2.cloned.1.call-done, f32[80,80]{1,0:T(8,128)S(1)} %get-tuple-element.6, s32[]{:T(128)S(6)} %select_n.3, f32[5]{0:T(128)S(1)} %dynamic-slice), kind=kOutput, calls=%fused_computation.20 | convolution fusion | flops 19784480 | bytes 4182532 | tf_op jit(solution)/shard_map/mn,ncwh->mcwh/dot_general | solution.py:69
  193.5 7.6 %collective-permute-start.2 = (bf16[5,24,1,128]{3,0,2,1:T(8,128)(2,1)S(1)}, bf16[5,24,1,128]{3,0,2,1:T(8,128)(2,1)S(1)}, u32[]{:S(2)}, u32[]{:S(2)}) collective-permute-start(bf16[5,24,1,128]{3,0,2,1:T(8,128)(2,1)S(1)} %get-tuple-element.27), channel_id=1, source_target_pairs={{0,1},{1,2},{2,3},{3,4},{4,5},{5,6},{6,7},{7,8},{8,9},{9,10},{10,1... | collective-permute-start | bytes 92168 | tf_op jit(solution)/shard_map/ppermute | solution.py:14
  201.2 2.1 collective-permute-start.3
  203.3 7.6 %collective-permute-done.3 = bf16[5,24,1,128]{3,0,2,1:T(8,128)(2,1)S(1)} collective-permute-done((bf16[5,24,1,128]{3,0,2,1:T(8,128)(2,1)S(1)}, bf16[5,24,1,128]{3,0,2,1:T(8,128)(2,1)S(1)}, u32[]{:S(2)}, u32[]{:S(2)}) %collective-permute-start.3) | collective-permute-done | bytes 30752 | tf_op jit(solution)/shard_map/ppermute | solution.py:17
  212.8 2.6 %fusion.17 = bf16[5,64,8,128]{3,1,2,0:T(8,128)(2,1)S(1)} fusion(bf16[5,216,8,128]{3,0,2,1:T(8,128)(2,1)S(1)} %slice_dynamic-update-slice_fusion.6, bf16[64,216]{1,0:T(8,128)(2,1)S(1)} %copy-done, bf16[5,64,8,128]{3,2,1,0:T(8,128)(2,1)S(1)} %copy-done.1), kind=kOutput, calls=%fused_computation.18 | convolution fusion | flops 142540800 | bytes 3550208 | tf_op jit(solution)/shard_map/oc,mcwh->mowh/dot_general | solution.py:76
  215.4 1.3 copy.59
  (87 shorter events, 16.7 us)
Async XLA Ops:
  6.5 206.3 %copy-start = (bf16[64,216]{1,0:T(8,128)(2,1)S(1)}, bf16[64,216]{1,0:T(8,128)(2,1)}, u32[]{:S(2)}) copy-start(bf16[64,216]{1,0:T(8,128)(2,1)} %param.9) | copy-start | bytes 82948
  6.5 182.7 %all-gather.2.cloned.1.call-start = ((), (), s32[]{:S(2)}) async-start(), calls=%async_computation.2 | async-start | bytes 4177920 | tf_op jit(solution)/shard_map/all_gather | solution.py:72
  7.8 7.8 %collective-permute-start = (bf16[5,64,1,128]{3,1,2,0:T(8,128)(2,1)S(1)}, bf16[5,64,1,128]{3,1,2,0:T(8,128)(2,1)S(1)}, u32[]{:S(2)}, u32[]{:S(2)}) collective-permute-start(bf16[5,64,1,128]{3,1,2,0:T(8,128)(2,1)S(1)} %get-tuple-element.25), channel_id=1, source_target_pairs={{0,1},{1,2},{2,3},{3,4},{4,5},{5,6},{6,7},{7,8},{8,9},{9,10},{10,1... | collective-permute-start | bytes 245768 | tf_op jit(solution)/shard_map/ppermute | solution.py:14
  13.7 10.9 %collective-permute-start.1 = (bf16[5,64,1,128]{3,1,2,0:T(8,128)(2,1)S(1)}, bf16[5,64,1,128]{3,1,2,0:T(8,128)(2,1)S(1)}, u32[]{:S(2)}, u32[]{:S(2)}) collective-permute-start(bf16[5,64,1,128]{3,1,2,0:T(8,128)(2,1)S(1)} %get-tuple-element.26), channel_id=1, source_target_pairs={{1,0},{2,1},{3,2},{4,3},{5,4},{6,5},{7,6},{8,7},{9,8},{10,9},{11,1... | collective-permute-start | bytes 245768 | tf_op jit(solution)/shard_map/ppermute | solution.py:17
  25.6 1.1 copy-start.1
  27.3 0.8 copy-start.7
  27.3 0.8 copy-start.8
  27.3 0.8 copy-start.9
  33.1 7.8 %copy-start.3 = (bf16[1,5,24,8,8]{4,2,3,1,0:T(8,128)(2,1)S(1)}, bf16[1,5,24,8,8]{4,2,3,1,0:T(8,128)(2,1)}, u32[]{:S(2)}) copy-start(bf16[1,5,24,8,8]{4,2,3,1,0:T(8,128)(2,1)} %get-tuple-element.16) | copy-start | bytes 46084
  33.1 8.0 %copy-start.2 = (bf16[1,5,24,8,8]{4,2,3,1,0:T(8,128)(2,1)S(1)}, bf16[1,5,24,8,8]{4,2,3,1,0:T(8,128)(2,1)}, u32[]{:S(2)}) copy-start(bf16[1,5,24,8,8]{4,2,3,1,0:T(8,128)(2,1)} %get-tuple-element.15) | copy-start | bytes 46084
  41.1 1.4 copy-start.5
  41.1 1.5 copy-start.6
  42.7 12.8 %copy-start.4 = (bf16[5,24,8,128]{3,1,2,0:T(8,128)(2,1)S(1)}, bf16[5,24,8,128]{3,1,2,0:T(8,128)(2,1)}, u32[]{:S(2)}) copy-start(bf16[5,24,8,128]{3,1,2,0:T(8,128)(2,1)} %get-tuple-element.23) | copy-start | bytes 737284
  45.4 20.0 %all-to-all-start.1 = ((bf16[16,2,3840]{2,1,0:T(2,128)(2,1)}), bf16[16,2,3840]{2,1,0:T(2,128)(2,1)S(1)}, u32[]{:S(2)}, u32[]{:S(2)}) async-start(bf16[16,2,3840]{2,1,0:T(2,128)(2,1)} %reshape.12), calls=%async_computation.1 | async-start | bytes 491520 | tf_op jit(solution)/shard_map/all_to_all | solution.py:52
  65.4 15.4 %all-to-all-start = ((bf16[16,2,3840]{2,1,0:T(2,128)(2,1)}), bf16[16,2,3840]{2,1,0:T(2,128)(2,1)S(1)}, u32[]{:S(2)}, u32[]{:S(2)}) async-start(bf16[16,2,3840]{2,1,0:T(2,128)(2,1)} %reshape.10), calls=%async_computation | async-start | bytes 491520 | tf_op jit(solution)/shard_map/all_to_all | solution.py:50
  193.5 9.8 %collective-permute-start.2 = (bf16[5,24,1,128]{3,0,2,1:T(8,128)(2,1)S(1)}, bf16[5,24,1,128]{3,0,2,1:T(8,128)(2,1)S(1)}, u32[]{:S(2)}, u32[]{:S(2)}) collective-permute-start(bf16[5,24,1,128]{3,0,2,1:T(8,128)(2,1)S(1)} %get-tuple-element.27), channel_id=1, source_target_pairs={{0,1},{1,2},{2,3},{3,4},{4,5},{5,6},{6,7},{7,8},{8,9},{9,10},{10,1... | collective-permute-start | bytes 92168 | tf_op jit(solution)/shard_map/ppermute | solution.py:14
  201.2 9.7 %collective-permute-start.3 = (bf16[5,24,1,128]{3,0,2,1:T(8,128)(2,1)S(1)}, bf16[5,24,1,128]{3,0,2,1:T(8,128)(2,1)S(1)}, u32[]{:S(2)}, u32[]{:S(2)}) collective-permute-start(bf16[5,24,1,128]{3,0,2,1:T(8,128)(2,1)S(1)} %get-tuple-element.28), channel_id=1, source_target_pairs={{1,0},{2,1},{3,2},{4,3},{5,4},{6,5},{7,6},{8,7},{9,8},{10,9},{11,1... | collective-permute-start | bytes 92168 | tf_op jit(solution)/shard_map/ppermute | solution.py:17
Sparse Core Ops, SparseCore 0:
  30.9 105.0 all-gather.1
